TPU v7x, 32 devices: a whole 2x2x4 slice. The times are simulated.
32 devices in a mesh: groups: 2 (over x), slab: 16 (over z, y, core).
Axes of the slice: x: 2, y: 2, z: 4, core: 2. Of those that a mesh axis runs over, the one named last changes fastest.
Arguments:
- queries: bfloat16 [32, 8192], P(('groups', 'slab')), parts along dimension 0, may hold values from -40 to 40
- prefix_keys: bfloat16 [32768, 1024], P(('groups', 'slab')), parts along dimension 0, may hold values from -5 to 5
- prefix_values: bfloat16 [32768, 1024], P(('groups', 'slab')), parts along dimension 0, may hold values from -6 to 6
- block_ids: int32 [32, 32], P('groups'), parts along dimension 0, may hold values from 0 to 127, as said below
Outputs:
- attended: bfloat16 [32, 8192], P(('groups', 'slab')), parts along dimension 0
- log_totals: float32 [32, 64], P(('groups', 'slab')), parts along dimension 0
There are 2 independent parts, one for each index of `groups`. A program takes and returns all parts, laid end to end along the dimension named above; each array names one. Nothing has to cross between parts.
Inputs may be any that keep to these rules, and one draw needn't show every extreme that they name: `block_ids`: each row names 32 different blocks of the 128 in rising order.
All inputs are finite; a program needn't handle non-finite values.
Results may differ from a plain program's by a relative error of at most 0.0065.
Values may be sent and summed in bfloat16 or wider, within the bound.
A program may use at most 64 MiB of HBM per device.

v0:
```python
import math

import jax
import jax.numpy as jnp
from jax import lax
from jax.sharding import PartitionSpec as P

HD = 128
BLOCK = 128


masked_score = -1e30


def block_bias(chosen, first_block, blocks_here):
    local_blocks = first_block + jnp.arange(blocks_here, dtype=jnp.int32)
    present = jnp.any(chosen[..., :, None] == local_blocks, axis=-2)
    present = jnp.repeat(present, BLOCK, axis=-1)
    return jnp.where(present, 0.0, masked_score).astype(jnp.float32)


def local_partial(query_rows, key_cols, value_cols, bias_rows):
    rows = query_rows.shape[0]
    groups = key_cols.shape[1] // HD
    span = key_cols.shape[0]
    per_group = query_rows.shape[1] // (groups * HD)
    head_rows = query_rows.reshape(rows, groups, per_group, HD)
    key_heads = key_cols.reshape(span, groups, HD)
    value_heads = value_cols.reshape(span, groups, HD)
    scores = jnp.einsum(
        "rkgd,lkd->rkgl", head_rows, key_heads, preferred_element_type=jnp.float32
    ) * (1.0 / math.sqrt(HD))
    scores = scores + bias_rows[:, None, None, :]
    row_max = jnp.max(scores, axis=-1)
    weights = jnp.exp(scores - row_max[..., None])
    row_total = jnp.sum(weights, axis=-1)
    mixed_sum = jnp.einsum(
        "rkgl,lkd->rkgd",
        weights.astype(jnp.bfloat16),
        value_heads,
        preferred_element_type=jnp.float32,
    )
    return (
        row_max.reshape(rows, groups * per_group),
        row_total.reshape(rows, groups * per_group),
        mixed_sum.reshape(rows, groups * per_group * HD),
    )


def finish(state):
    rows, heads = state[0].shape
    output = (state[2].reshape(rows, heads, HD) / state[1][..., None]).reshape(rows, heads * HD)
    return (output.astype(jnp.bfloat16), state[0] + jnp.log(state[1]))


def merge_slabs(back_max, back_total, back_sum, rows, heads_all, width):
    slab_count = back_max.shape[0]
    joint = jnp.max(back_max, axis=0)
    factors = jnp.exp(back_max - joint[None])
    totals = jnp.sum(back_total * factors, axis=0)
    sums = jnp.sum(back_sum.reshape(slab_count, rows, heads_all, HD) * factors[..., None], axis=0)
    return (joint, totals, sums.reshape(rows, width))


def shards(queries, prefix_keys, prefix_values, block_ids):
    own_index = lax.axis_index("slab")
    slab_count = lax.axis_size("slab")
    rows = queries.shape[0]
    width = queries.shape[1]
    heads_all = width // HD
    blocks_here = prefix_keys.shape[0] // BLOCK
    first_block = own_index * blocks_here
    chosen_all = block_ids.reshape(slab_count, rows, block_ids.shape[1])
    everyone = lax.all_gather(queries, "slab", axis=0, tiled=True)
    grouped = everyone.reshape(slab_count, rows, width)
    owner_bias = block_bias(chosen_all, first_block, blocks_here)

    def per_owner(request):
        return local_partial(request[0], prefix_keys, prefix_values, request[1])

    part_max, part_total, part_sum = lax.map(per_owner, (grouped, owner_bias))
    back_max, back_total, back_sum = (
        lax.all_to_all(part_max, "slab", split_axis=0, concat_axis=0, tiled=True),
        lax.all_to_all(part_total, "slab", split_axis=0, concat_axis=0, tiled=True),
        lax.all_to_all(part_sum, "slab", split_axis=0, concat_axis=0, tiled=True),
    )
    state = merge_slabs(back_max, back_total, back_sum, rows, heads_all, width)
    attended, log_totals = finish(state)
    return (attended, log_totals)


def solution(mesh):
    in_specs = (
        P(("groups", "slab"), None),
        P(("groups", "slab"), None),
        P(("groups", "slab"), None),
        P("groups", None),
    )
    out_specs = (P(("groups", "slab"), None), P(("groups", "slab"), None))
    return jax.shard_map(shards, mesh=mesh, in_specs=in_specs, out_specs=out_specs, check_vma=False)
```

profile of v0, /device:TPU:0, one launch (start us, length us, event | category | flops | bytes accessed | tf_op | source)
XLA Modules:
  0.0 129.9 jit_solution(16083771346249900336)
XLA Ops:
  0.7 1.1 compare_reduce_fusion
  1.8 24.8 %all-gather = bf16[16,1,8192]{2,1,0:T(2,128)(2,1)S(1)} all-gather(bf16[1,1,8192]{2,1,0:T(2,128)(2,1)} %bitcast.81), channel_id=1, replica_groups=mesh['groups'=2,'slab'=16] {'slab'}, dimensions={0}, use_global_device_ids=true | all-gather | bytes 278528 | tf_op jit(solution)/shard_map/all_gather | solution.py:74
  26.7 65.6 %while.14 = (s32[]{:T(128)}, f32[16,1,64]{2,1,0:T(1,128)S(1)}, f32[16,1,64]{2,1,0:T(1,128)S(1)}, f32[16,1,8192]{2,1,0:T(1,128)}, bf16[16,1,8192]{2,1,0:T(2,128)(...) while((s32[]{:T(128)}, f32[16,1,64]{2,1,0:T(1,128)S(1)}, ...), condition=%wide.region_4.5_spmd, body=%wide.region_1.4_spmd.sunk | while | flops 34013056 | bytes 13533329 | solution.py:81
  26.8 2.4 %fusion.38 = (f32[8,8]{1,0:T(8,128)S(1)}, f32[1,8,8,1024]{3,2,1,0:T(8,128)S(1)}) fusion(f32[1024]{0:T(1024)S(1)} %bitcast.76, bf16[8192]{0:T(1024)(128)(2,1)S(1)} %dynamic-slice_reduce_fusion.2, bf16[1024,1024]{1,0:T(8,128)(2,1)} %get-tuple-element.151), kind=kOutput, calls=%fused_computation.29.clone.1 | convolution fusion | flops 16973760 | bytes 2380032 | tf_op jit(solution)/shard_map/while/body/eval_jaxpr/rkgd,lkd->rkgl/dot_general | solution.py:30
  30.9 2.4 %fusion.38 = (f32[8,8]{1,0:T(8,128)S(1)}, f32[1,8,8,1024]{3,2,1,0:T(8,128)S(1)}) fusion(f32[1024]{0:T(1024)S(1)} %bitcast.76, bf16[8192]{0:T(1024)(128)(2,1)S(1)} %dynamic-slice_reduce_fusion.2, bf16[1024,1024]{1,0:T(8,128)(2,1)} %get-tuple-element.151), kind=kOutput, calls=%fused_computation.29.clone.1 | convolution fusion | flops 16973760 | bytes 2380032 | tf_op jit(solution)/shard_map/while/body/eval_jaxpr/rkgd,lkd->rkgl/dot_general | solution.py:30
  35.0 2.4 %fusion.38 = (f32[8,8]{1,0:T(8,128)S(1)}, f32[1,8,8,1024]{3,2,1,0:T(8,128)S(1)}) fusion(f32[1024]{0:T(1024)S(1)} %bitcast.76, bf16[8192]{0:T(1024)(128)(2,1)S(1)} %dynamic-slice_reduce_fusion.2, bf16[1024,1024]{1,0:T(8,128)(2,1)} %get-tuple-element.151), kind=kOutput, calls=%fused_computation.29.clone.1 | convolution fusion | flops 16973760 | bytes 2380032 | tf_op jit(solution)/shard_map/while/body/eval_jaxpr/rkgd,lkd->rkgl/dot_general | solution.py:30
  39.1 2.4 %fusion.38 = (f32[8,8]{1,0:T(8,128)S(1)}, f32[1,8,8,1024]{3,2,1,0:T(8,128)S(1)}) fusion(f32[1024]{0:T(1024)S(1)} %bitcast.76, bf16[8192]{0:T(1024)(128)(2,1)S(1)} %dynamic-slice_reduce_fusion.2, bf16[1024,1024]{1,0:T(8,128)(2,1)} %get-tuple-element.151), kind=kOutput, calls=%fused_computation.29.clone.1 | convolution fusion | flops 16973760 | bytes 2380032 | tf_op jit(solution)/shard_map/while/body/eval_jaxpr/rkgd,lkd->rkgl/dot_general | solution.py:30
  43.2 2.4 %fusion.38 = (f32[8,8]{1,0:T(8,128)S(1)}, f32[1,8,8,1024]{3,2,1,0:T(8,128)S(1)}) fusion(f32[1024]{0:T(1024)S(1)} %bitcast.76, bf16[8192]{0:T(1024)(128)(2,1)S(1)} %dynamic-slice_reduce_fusion.2, bf16[1024,1024]{1,0:T(8,128)(2,1)} %get-tuple-element.151), kind=kOutput, calls=%fused_computation.29.clone.1 | convolution fusion | flops 16973760 | bytes 2380032 | tf_op jit(solution)/shard_map/while/body/eval_jaxpr/rkgd,lkd->rkgl/dot_general | solution.py:30
  47.3 2.4 %fusion.38 = (f32[8,8]{1,0:T(8,128)S(1)}, f32[1,8,8,1024]{3,2,1,0:T(8,128)S(1)}) fusion(f32[1024]{0:T(1024)S(1)} %bitcast.76, bf16[8192]{0:T(1024)(128)(2,1)S(1)} %dynamic-slice_reduce_fusion.2, bf16[1024,1024]{1,0:T(8,128)(2,1)} %get-tuple-element.151), kind=kOutput, calls=%fused_computation.29.clone.1 | convolution fusion | flops 16973760 | bytes 2380032 | tf_op jit(solution)/shard_map/while/body/eval_jaxpr/rkgd,lkd->rkgl/dot_general | solution.py:30
  51.4 2.4 %fusion.38 = (f32[8,8]{1,0:T(8,128)S(1)}, f32[1,8,8,1024]{3,2,1,0:T(8,128)S(1)}) fusion(f32[1024]{0:T(1024)S(1)} %bitcast.76, bf16[8192]{0:T(1024)(128)(2,1)S(1)} %dynamic-slice_reduce_fusion.2, bf16[1024,1024]{1,0:T(8,128)(2,1)} %get-tuple-element.151), kind=kOutput, calls=%fused_computation.29.clone.1 | convolution fusion | flops 16973760 | bytes 2380032 | tf_op jit(solution)/shard_map/while/body/eval_jaxpr/rkgd,lkd->rkgl/dot_general | solution.py:30
  55.5 2.4 %fusion.38 = (f32[8,8]{1,0:T(8,128)S(1)}, f32[1,8,8,1024]{3,2,1,0:T(8,128)S(1)}) fusion(f32[1024]{0:T(1024)S(1)} %bitcast.76, bf16[8192]{0:T(1024)(128)(2,1)S(1)} %dynamic-slice_reduce_fusion.2, bf16[1024,1024]{1,0:T(8,128)(2,1)} %get-tuple-element.151), kind=kOutput, calls=%fused_computation.29.clone.1 | convolution fusion | flops 16973760 | bytes 2380032 | tf_op jit(solution)/shard_map/while/body/eval_jaxpr/rkgd,lkd->rkgl/dot_general | solution.py:30
  59.6 2.4 %fusion.38 = (f32[8,8]{1,0:T(8,128)S(1)}, f32[1,8,8,1024]{3,2,1,0:T(8,128)S(1)}) fusion(f32[1024]{0:T(1024)S(1)} %bitcast.76, bf16[8192]{0:T(1024)(128)(2,1)S(1)} %dynamic-slice_reduce_fusion.2, bf16[1024,1024]{1,0:T(8,128)(2,1)} %get-tuple-element.151), kind=kOutput, calls=%fused_computation.29.clone.1 | convolution fusion | flops 16973760 | bytes 2380032 | tf_op jit(solution)/shard_map/while/body/eval_jaxpr/rkgd,lkd->rkgl/dot_general | solution.py:30
  63.7 2.4 %fusion.38 = (f32[8,8]{1,0:T(8,128)S(1)}, f32[1,8,8,1024]{3,2,1,0:T(8,128)S(1)}) fusion(f32[1024]{0:T(1024)S(1)} %bitcast.76, bf16[8192]{0:T(1024)(128)(2,1)S(1)} %dynamic-slice_reduce_fusion.2, bf16[1024,1024]{1,0:T(8,128)(2,1)} %get-tuple-element.151), kind=kOutput, calls=%fused_computation.29.clone.1 | convolution fusion | flops 16973760 | bytes 2380032 | tf_op jit(solution)/shard_map/while/body/eval_jaxpr/rkgd,lkd->rkgl/dot_general | solution.py:30
  67.8 2.4 %fusion.38 = (f32[8,8]{1,0:T(8,128)S(1)}, f32[1,8,8,1024]{3,2,1,0:T(8,128)S(1)}) fusion(f32[1024]{0:T(1024)S(1)} %bitcast.76, bf16[8192]{0:T(1024)(128)(2,1)S(1)} %dynamic-slice_reduce_fusion.2, bf16[1024,1024]{1,0:T(8,128)(2,1)} %get-tuple-element.151), kind=kOutput, calls=%fused_computation.29.clone.1 | convolution fusion | flops 16973760 | bytes 2380032 | tf_op jit(solution)/shard_map/while/body/eval_jaxpr/rkgd,lkd->rkgl/dot_general | solution.py:30
  71.9 2.4 %fusion.38 = (f32[8,8]{1,0:T(8,128)S(1)}, f32[1,8,8,1024]{3,2,1,0:T(8,128)S(1)}) fusion(f32[1024]{0:T(1024)S(1)} %bitcast.76, bf16[8192]{0:T(1024)(128)(2,1)S(1)} %dynamic-slice_reduce_fusion.2, bf16[1024,1024]{1,0:T(8,128)(2,1)} %get-tuple-element.151), kind=kOutput, calls=%fused_computation.29.clone.1 | convolution fusion | flops 16973760 | bytes 2380032 | tf_op jit(solution)/shard_map/while/body/eval_jaxpr/rkgd,lkd->rkgl/dot_general | solution.py:30
  76.0 2.4 %fusion.38 = (f32[8,8]{1,0:T(8,128)S(1)}, f32[1,8,8,1024]{3,2,1,0:T(8,128)S(1)}) fusion(f32[1024]{0:T(1024)S(1)} %bitcast.76, bf16[8192]{0:T(1024)(128)(2,1)S(1)} %dynamic-slice_reduce_fusion.2, bf16[1024,1024]{1,0:T(8,128)(2,1)} %get-tuple-element.151), kind=kOutput, calls=%fused_computation.29.clone.1 | convolution fusion | flops 16973760 | bytes 2380032 | tf_op jit(solution)/shard_map/while/body/eval_jaxpr/rkgd,lkd->rkgl/dot_general | solution.py:30
  80.1 2.4 %fusion.38 = (f32[8,8]{1,0:T(8,128)S(1)}, f32[1,8,8,1024]{3,2,1,0:T(8,128)S(1)}) fusion(f32[1024]{0:T(1024)S(1)} %bitcast.76, bf16[8192]{0:T(1024)(128)(2,1)S(1)} %dynamic-slice_reduce_fusion.2, bf16[1024,1024]{1,0:T(8,128)(2,1)} %get-tuple-element.151), kind=kOutput, calls=%fused_computation.29.clone.1 | convolution fusion | flops 16973760 | bytes 2380032 | tf_op jit(solution)/shard_map/while/body/eval_jaxpr/rkgd,lkd->rkgl/dot_general | solution.py:30
  84.2 2.4 %fusion.38 = (f32[8,8]{1,0:T(8,128)S(1)}, f32[1,8,8,1024]{3,2,1,0:T(8,128)S(1)}) fusion(f32[1024]{0:T(1024)S(1)} %bitcast.76, bf16[8192]{0:T(1024)(128)(2,1)S(1)} %dynamic-slice_reduce_fusion.2, bf16[1024,1024]{1,0:T(8,128)(2,1)} %get-tuple-element.151), kind=kOutput, calls=%fused_computation.29.clone.1 | convolution fusion | flops 16973760 | bytes 2380032 | tf_op jit(solution)/shard_map/while/body/eval_jaxpr/rkgd,lkd->rkgl/dot_general | solution.py:30
  88.3 2.4 %fusion.38 = (f32[8,8]{1,0:T(8,128)S(1)}, f32[1,8,8,1024]{3,2,1,0:T(8,128)S(1)}) fusion(f32[1024]{0:T(1024)S(1)} %bitcast.76, bf16[8192]{0:T(1024)(128)(2,1)S(1)} %dynamic-slice_reduce_fusion.2, bf16[1024,1024]{1,0:T(8,128)(2,1)} %get-tuple-element.151), kind=kOutput, calls=%fused_computation.29.clone.1 | convolution fusion | flops 16973760 | bytes 2380032 | tf_op jit(solution)/shard_map/while/body/eval_jaxpr/rkgd,lkd->rkgl/dot_general | solution.py:30
  92.2 9.0 %all_to_all.15 = f32[16,1,64]{2,1,0:T(1,128)S(1)} all-to-all(f32[16,1,64]{2,1,0:T(1,128)S(1)} %get-tuple-element.47), channel_id=1, replica_groups=mesh['groups'=2,'slab'=16] {'slab'}, dimensions={0} | all-to-all | bytes 8192 | tf_op jit(solution)/shard_map/all_to_all | solution.py:83
  101.2 9.0 %all_to_all.16 = f32[16,1,64]{2,1,0:T(1,128)S(1)} all-to-all(f32[16,1,64]{2,1,0:T(1,128)S(1)} %get-tuple-element.48), channel_id=1, replica_groups=mesh['groups'=2,'slab'=16] {'slab'}, dimensions={0} | all-to-all | bytes 8192 | tf_op jit(solution)/shard_map/all_to_all | solution.py:84
  110.2 3.6 %all-to-all-start = ((f32[16,1,8192]{2,1,0:T(1,128)}), f32[16,1,8192]{2,1,0:T(1,128)S(1)}, u32[]{:S(2)}, u32[]{:S(2)}) async-start(f32[16,1,8192]{2,1,0:T(1,128)} %get-tuple-element.46), calls=%async_computation | async-start | bytes 1048576 | tf_op jit(solution)/shard_map/all_to_all | solution.py:85
  114.4 13.8 %all-to-all-done = f32[16,1,8192]{2,1,0:T(1,128)S(1)} async-done(((f32[16,1,8192]{2,1,0:T(1,128)}), f32[16,1,8192]{2,1,0:T(1,128)S(1)}, u32[]{:S(2)}, u32[]{:S(2)}) %all-to-all-start) | async-done | bytes 524320 | tf_op jit(solution)/shard_map/all_to_all | solution.py:85
  128.4 0.8 multiply_reduce_fusion
  (172 shorter events, 27.8 us)
Async XLA Ops:
  26.7 2.9 %copy-start = (bf16[1024,1024]{1,0:T(8,128)(2,1)S(1)}, bf16[1024,1024]{1,0:T(8,128)(2,1)}, u32[]{:S(2)}) copy-start(bf16[1024,1024]{1,0:T(8,128)(2,1)} %get-tuple-element.153) | copy-start | bytes 6291460 | tf_op jit(solution)/shard_map/while
  30.8 2.8 %copy-start = (bf16[1024,1024]{1,0:T(8,128)(2,1)S(1)}, bf16[1024,1024]{1,0:T(8,128)(2,1)}, u32[]{:S(2)}) copy-start(bf16[1024,1024]{1,0:T(8,128)(2,1)} %get-tuple-element.153) | copy-start | bytes 6291460 | tf_op jit(solution)/shard_map/while
  34.9 2.8 %copy-start = (bf16[1024,1024]{1,0:T(8,128)(2,1)S(1)}, bf16[1024,1024]{1,0:T(8,128)(2,1)}, u32[]{:S(2)}) copy-start(bf16[1024,1024]{1,0:T(8,128)(2,1)} %get-tuple-element.153) | copy-start | bytes 6291460 | tf_op jit(solution)/shard_map/while
  39.0 2.8 %copy-start = (bf16[1024,1024]{1,0:T(8,128)(2,1)S(1)}, bf16[1024,1024]{1,0:T(8,128)(2,1)}, u32[]{:S(2)}) copy-start(bf16[1024,1024]{1,0:T(8,128)(2,1)} %get-tuple-element.153) | copy-start | bytes 6291460 | tf_op jit(solution)/shard_map/while
  43.1 2.8 %copy-start = (bf16[1024,1024]{1,0:T(8,128)(2,1)S(1)}, bf16[1024,1024]{1,0:T(8,128)(2,1)}, u32[]{:S(2)}) copy-start(bf16[1024,1024]{1,0:T(8,128)(2,1)} %get-tuple-element.153) | copy-start | bytes 6291460 | tf_op jit(solution)/shard_map/while
  47.2 2.8 %copy-start = (bf16[1024,1024]{1,0:T(8,128)(2,1)S(1)}, bf16[1024,1024]{1,0:T(8,128)(2,1)}, u32[]{:S(2)}) copy-start(bf16[1024,1024]{1,0:T(8,128)(2,1)} %get-tuple-element.153) | copy-start | bytes 6291460 | tf_op jit(solution)/shard_map/while
  51.3 2.8 %copy-start = (bf16[1024,1024]{1,0:T(8,128)(2,1)S(1)}, bf16[1024,1024]{1,0:T(8,128)(2,1)}, u32[]{:S(2)}) copy-start(bf16[1024,1024]{1,0:T(8,128)(2,1)} %get-tuple-element.153) | copy-start | bytes 6291460 | tf_op jit(solution)/shard_map/while
  55.4 2.8 %copy-start = (bf16[1024,1024]{1,0:T(8,128)(2,1)S(1)}, bf16[1024,1024]{1,0:T(8,128)(2,1)}, u32[]{:S(2)}) copy-start(bf16[1024,1024]{1,0:T(8,128)(2,1)} %get-tuple-element.153) | copy-start | bytes 6291460 | tf_op jit(solution)/shard_map/while
  59.5 2.8 %copy-start = (bf16[1024,1024]{1,0:T(8,128)(2,1)S(1)}, bf16[1024,1024]{1,0:T(8,128)(2,1)}, u32[]{:S(2)}) copy-start(bf16[1024,1024]{1,0:T(8,128)(2,1)} %get-tuple-element.153) | copy-start | bytes 6291460 | tf_op jit(solution)/shard_map/while
  63.6 2.8 %copy-start = (bf16[1024,1024]{1,0:T(8,128)(2,1)S(1)}, bf16[1024,1024]{1,0:T(8,128)(2,1)}, u32[]{:S(2)}) copy-start(bf16[1024,1024]{1,0:T(8,128)(2,1)} %get-tuple-element.153) | copy-start | bytes 6291460 | tf_op jit(solution)/shard_map/while
  67.7 2.8 %copy-start = (bf16[1024,1024]{1,0:T(8,128)(2,1)S(1)}, bf16[1024,1024]{1,0:T(8,128)(2,1)}, u32[]{:S(2)}) copy-start(bf16[1024,1024]{1,0:T(8,128)(2,1)} %get-tuple-element.153) | copy-start | bytes 6291460 | tf_op jit(solution)/shard_map/while
  71.8 2.8 %copy-start = (bf16[1024,1024]{1,0:T(8,128)(2,1)S(1)}, bf16[1024,1024]{1,0:T(8,128)(2,1)}, u32[]{:S(2)}) copy-start(bf16[1024,1024]{1,0:T(8,128)(2,1)} %get-tuple-element.153) | copy-start | bytes 6291460 | tf_op jit(solution)/shard_map/while
  75.9 2.8 %copy-start = (bf16[1024,1024]{1,0:T(8,128)(2,1)S(1)}, bf16[1024,1024]{1,0:T(8,128)(2,1)}, u32[]{:S(2)}) copy-start(bf16[1024,1024]{1,0:T(8,128)(2,1)} %get-tuple-element.153) | copy-start | bytes 6291460 | tf_op jit(solution)/shard_map/while
  80.0 2.8 %copy-start = (bf16[1024,1024]{1,0:T(8,128)(2,1)S(1)}, bf16[1024,1024]{1,0:T(8,128)(2,1)}, u32[]{:S(2)}) copy-start(bf16[1024,1024]{1,0:T(8,128)(2,1)} %get-tuple-element.153) | copy-start | bytes 6291460 | tf_op jit(solution)/shard_map/while
  84.1 2.8 %copy-start = (bf16[1024,1024]{1,0:T(8,128)(2,1)S(1)}, bf16[1024,1024]{1,0:T(8,128)(2,1)}, u32[]{:S(2)}) copy-start(bf16[1024,1024]{1,0:T(8,128)(2,1)} %get-tuple-element.153) | copy-start | bytes 6291460 | tf_op jit(solution)/shard_map/while
  88.1 2.8 %copy-start = (bf16[1024,1024]{1,0:T(8,128)(2,1)S(1)}, bf16[1024,1024]{1,0:T(8,128)(2,1)}, u32[]{:S(2)}) copy-start(bf16[1024,1024]{1,0:T(8,128)(2,1)} %get-tuple-element.153) | copy-start | bytes 6291460 | tf_op jit(solution)/shard_map/while
  110.2 18.0 %all-to-all-start = ((f32[16,1,8192]{2,1,0:T(1,128)}), f32[16,1,8192]{2,1,0:T(1,128)S(1)}, u32[]{:S(2)}, u32[]{:S(2)}) async-start(f32[16,1,8192]{2,1,0:T(1,128)} %get-tuple-element.46), calls=%async_computation | async-start | bytes 1048576 | tf_op jit(solution)/shard_map/all_to_all | solution.py:85
where the time goes:
time: 130 us
  matrix products  47.9 us (37%)
  blocking collectives  42.7 us (33%)
  local copies, waits for them, and re-layouts  14.5 us (11%)
  waiting for transfers between devices  13.8 us (11%)
  other arithmetic  6.35 us (5%)
  starting transfers between devices  3.57 us (3%)
    dot_general x16, matrix products, local_partial(): jnp.einsum('rkgd,lkd->rkgl', head_rows, key_heads, preferred_element_type...  39.2 us
    all_gather x1, blocking collectives, shards(): everyone = lax.all_gather(queries, 'slab', axis=0, tiled=True)  24.8 us
    all_to_all x1, waiting for transfers between devices, shards(): lax.all_to_all(part_sum, 'slab', split_axis=0, concat_axis=0, tiled=True)  13.8 us
    dynamic_update_slice x32, local copies, waits for them, and re-layouts, shards(): part_max, part_total, part_sum = lax.map(per_owner, (grouped, owner_bias))  10 us
    all_to_all x1, blocking collectives, shards(): lax.all_to_all(part_total, 'slab', split_axis=0, concat_axis=0, tiled=True)  8.97 us
    all_to_all x1, blocking collectives, shards(): lax.all_to_all(part_max, 'slab', split_axis=0, concat_axis=0, tiled=True)  8.97 us
    dot_general x16, matrix products, local_partial(): jnp.einsum('rkgl,lkd->rkgd', weights.astype(jnp.bfloat16), value_heads, p...  8.76 us
    all_to_all x1, starting transfers between devices, shards(): lax.all_to_all(part_sum, 'slab', split_axis=0, concat_axis=0, tiled=True)  3.57 us
  transfers between devices with their start and end apart: 1, of which 1 were waited for; matrix products, arithmetic and copies ran while one was open for 0% of the time, Pallas kernels for 0%

commit v1 on v0

v1 whole, which is shorter than its diff:
```python
import functools
import math

import jax
import jax.numpy as jnp
from jax import lax
from jax.experimental import pallas as pl
from jax.experimental.pallas import tpu as pltpu
from jax.sharding import PartitionSpec as P

HD = 128
BLOCK = 128
SUB = 8
TILE = 16
CHUNK = 16
MESH = pl.DeviceIdType.MESH

masked_score = -1e30


def kernel(
    n, q_hbm, k_hbm, v_hbm, ids_hbm, att_ref, log_ref,
    q_raw, q_own, ids, kbuf, vbuf, held, bias, out, out_stat, got, got_stat,
    load_sem, q_send, q_recv, o_send, o_recv, s_send, s_recv,
):
    me = lax.axis_index("slab")
    heads = q_own.shape[0]
    kv_heads = kbuf.shape[1] // HD
    pairs = heads // TILE
    span = kbuf.shape[0]
    blocks_here = span // BLOCK
    chunk = min(CHUNK, n)
    chunks = n // chunk
    factor = 1.0 / math.sqrt(HD)
    factor2 = factor * math.log2(math.e)

    barrier = pltpu.get_barrier_semaphore()

    def peer_of(i):
        return lax.rem(me + i, n)

    @pl.loop(1, n)
    def _(i):
        pl.semaphore_signal(barrier, inc=1, device_id={"slab": peer_of(i)}, device_id_type=MESH)

    loads = [
        pltpu.make_async_copy(src, dst, load_sem.at[at])
        for at, (src, dst) in enumerate(((q_hbm, q_raw), (ids_hbm, ids), (k_hbm, kbuf), (v_hbm, vbuf)))
    ]
    for load in loads:
        load.start()

    loads[0].wait()
    row = q_raw[...].astype(jnp.float32)
    q_own[...] = jnp.concatenate(
        [row[:, h * HD : (h + 1) * HD] for h in range(heads)], axis=0
    ).astype(jnp.bfloat16)

    pl.semaphore_wait(barrier, n - 1)

    @pl.loop(1, n)
    def _(i):
        pltpu.make_async_remote_copy(
            src_ref=q_own, dst_ref=held.at[me], send_sem=q_send, recv_sem=q_recv,
            device_id={"slab": peer_of(i)}, device_id_type=MESH,
        ).start()

    held[me] = q_own[...]

    loads[1].wait()

    def fill_bias(c):
        rows = pl.ds(c * chunk, chunk)
        wide = jnp.broadcast_to(ids[rows][:, None, :], (chunk, SUB, ids.shape[1]))
        for j in range(blocks_here):
            hit = jnp.where(wide == me * blocks_here + j, 0.0, masked_score)
            hit = jnp.max(hit, axis=-1, keepdims=True)
            bias[rows, :, j * BLOCK : (j + 1) * BLOCK] = jnp.broadcast_to(hit, (chunk, SUB, BLOCK))

    def each_chunk(body):
        if chunks == 1:
            body(0)
        else:
            pl.loop(0, chunks)(body)

    each_chunk(fill_bias)
    loads[2].wait()
    loads[3].wait()

    def whole(ref_at, send, recv):
        return pltpu.make_async_remote_copy(
            src_ref=ref_at, dst_ref=ref_at, send_sem=send, recv_sem=recv,
            device_id={"slab": peer_of(1)}, device_id_type=MESH,
        )

    others = pl.ds(0, n - 1)
    whole(held.at[others], q_send, q_recv).wait_recv()

    lane = lax.broadcasted_iota(jnp.int32, (chunk, SUB, HD), 2)
    sub = lax.broadcasted_iota(jnp.int32, (chunk * TILE, HD), 0)
    first = (lax.rem(sub, TILE) < SUB).astype(jnp.float32).astype(jnp.bfloat16)
    second = (lax.rem(sub, TILE) >= SUB).astype(jnp.float32).astype(jnp.bfloat16)

    for p in range(pairs):
        rows16 = slice(TILE * p, TILE * (p + 1))
        cols = slice(2 * HD * p, 2 * HD * (p + 1))

        def partial(c, p=p, rows16=rows16, cols=cols):
            rows = pl.ds(c * chunk, chunk)
            q = held[rows, rows16, :].reshape(chunk * TILE, HD)
            q = jnp.concatenate([q * first, q * second], axis=1)
            scores = lax.dot_general(
                q, kbuf[:, cols], (((1,), (1,)), ((), ())), preferred_element_type=jnp.float32
            ).reshape(chunk, 2, SUB, span)
            scores = scores + bias[rows][:, None]
            peak = jnp.max(scores, axis=-1, keepdims=True)
            weights = jnp.exp2((scores - peak) * factor2)
            total = jnp.sum(weights, axis=-1, keepdims=True)
            mixed = jnp.dot(
                weights.astype(jnp.bfloat16).reshape(chunk * TILE, span), vbuf[:, cols],
                preferred_element_type=jnp.float32,
            ).reshape(chunk, 2, SUB, 2 * HD)
            mixed = jnp.concatenate([mixed[:, 0:1, :, :HD], mixed[:, 1:2, :, HD:]], axis=1) / total
            out[rows, rows16, :] = mixed.reshape(chunk, TILE, HD).astype(jnp.bfloat16)
            logs = peak * factor + jnp.log(total)
            stat = jnp.zeros((chunk, SUB, HD), jnp.float32) if p == 0 else out_stat[rows]
            stat = jnp.where(lane == 2 * p, logs[:, 0], stat)
            out_stat[rows] = jnp.where(lane == 2 * p + 1, logs[:, 1], stat)

        each_chunk(partial)

        @pl.loop(1, n)
        def _(i, p=p, rows16=rows16):
            peer = peer_of(i)
            pltpu.make_async_remote_copy(
                src_ref=out.at[peer, rows16], dst_ref=got.at[me, rows16],
                send_sem=o_send.at[p], recv_sem=o_recv.at[p],
                device_id={"slab": peer}, device_id_type=MESH,
            ).start()

    @pl.loop(1, n)
    def _(i):
        peer = peer_of(i)
        pltpu.make_async_remote_copy(
            src_ref=out_stat.at[peer], dst_ref=got_stat.at[me], send_sem=s_send, recv_sem=s_recv,
            device_id={"slab": peer}, device_id_type=MESH,
        ).start()

    got[me] = out[me]
    got_stat[me] = out_stat[me]

    whole(got_stat.at[others], s_send, s_recv).wait_recv()
    logs = got_stat[...]
    peak = jnp.max(logs, axis=0)
    shares = jnp.exp(logs - peak[None])
    total = jnp.sum(shares, axis=0)
    shares = shares / total[None]
    joint = peak + jnp.log(total)

    head_lane = lax.broadcasted_iota(jnp.int32, (SUB, heads), 1)
    head_sub = lax.broadcasted_iota(jnp.int32, (SUB, heads), 0)
    spread = jnp.zeros((SUB, heads), jnp.float32)
    for k in range(kv_heads):
        spread = jnp.where(head_lane // SUB == k, joint[:, k : k + 1], spread)
    spread = jnp.where(lax.rem(head_lane, SUB) == head_sub, spread, 0.0)
    log_ref[...] = jnp.sum(spread, axis=0, keepdims=True)

    for p in range(pairs):
        rows16 = slice(TILE * p, TILE * (p + 1))
        whole(got.at[others, rows16], o_send.at[p], o_recv.at[p]).wait_recv()
        parts = got[:, rows16, :].astype(jnp.float32).reshape(n, 2, SUB, HD)
        merged = [
            jnp.sum(parts[:, half] * shares[:, :, 2 * p + half : 2 * p + half + 1], axis=0) for half in range(2)
        ]
        att_ref[rows16, :] = jnp.concatenate(merged, axis=0).astype(jnp.bfloat16)

    whole(held.at[others], q_send, q_recv).wait_send()
    whole(got_stat.at[others], s_send, s_recv).wait_send()
    for p in range(pairs):
        rows16 = slice(TILE * p, TILE * (p + 1))
        whole(got.at[others, rows16], o_send.at[p], o_recv.at[p]).wait_send()


def shards(queries, prefix_keys, prefix_values, block_ids):
    n = lax.axis_size("slab")
    rows, width = queries.shape
    span, kv_width = prefix_keys.shape
    heads = width // HD
    pairs = heads // TILE
    assert rows == 1 and block_ids.shape[0] == n and heads == SUB * (kv_width // HD)
    anywhere = pl.BlockSpec(memory_space=pltpu.HBM)
    in_vmem = pl.BlockSpec(memory_space=pltpu.VMEM)
    attended, log_totals = pl.pallas_call(
        functools.partial(kernel, n),
        out_shape=(
            jax.ShapeDtypeStruct((heads, HD), jnp.bfloat16),
            jax.ShapeDtypeStruct((1, heads), jnp.float32),
        ),
        in_specs=[anywhere] * 4,
        out_specs=(in_vmem, in_vmem),
        scratch_shapes=[
            pltpu.VMEM((1, width), jnp.bfloat16),
            pltpu.VMEM((heads, HD), jnp.bfloat16),
            pltpu.VMEM(block_ids.shape, jnp.int32),
            pltpu.VMEM((span, kv_width), jnp.bfloat16),
            pltpu.VMEM((span, kv_width), jnp.bfloat16),
            pltpu.VMEM((n, heads, HD), jnp.bfloat16),
            pltpu.VMEM((n, SUB, span), jnp.float32),
            pltpu.VMEM((n, heads, HD), jnp.bfloat16),
            pltpu.VMEM((n, SUB, HD), jnp.float32),
            pltpu.VMEM((n, heads, HD), jnp.bfloat16),
            pltpu.VMEM((n, SUB, HD), jnp.float32),
            pltpu.SemaphoreType.DMA((4,)),
            pltpu.SemaphoreType.DMA,
            pltpu.SemaphoreType.DMA,
            pltpu.SemaphoreType.DMA((pairs,)),
            pltpu.SemaphoreType.DMA((pairs,)),
            pltpu.SemaphoreType.DMA,
            pltpu.SemaphoreType.DMA,
        ],
        compiler_params=pltpu.CompilerParams(
            collective_id=0, has_side_effects=True, vmem_limit_bytes=48 * 1024 * 1024
        ),
        cost_estimate=pl.CostEstimate(
            flops=8 * n * heads * span * HD,
            bytes_accessed=4 * span * kv_width,
            transcendentals=n * heads * span,
        ),
    )(queries, prefix_keys, prefix_values, block_ids)
    return attended.reshape(rows, width), log_totals


def solution(mesh):
    in_specs = (
        P(("groups", "slab"), None),
        P(("groups", "slab"), None),
        P(("groups", "slab"), None),
        P("groups", None),
    )
    out_specs = (P(("groups", "slab"), None), P(("groups", "slab"), None))
    return jax.shard_map(shards, mesh=mesh, in_specs=in_specs, out_specs=out_specs, check_vma=False)
```

time: 130 us -> 30.6 us (0.24)
  matrix products: 47.9 us -> 0 us
  blocking collectives: 42.7 us -> 0 us
  Pallas kernels: 0 us -> 23.8 us
  waiting for transfers between devices: 13.8 us -> 0 us
  local copies, waits for them, and re-layouts: 14.5 us -> 5.78 us
  other arithmetic: 6.35 us -> 0 us
  starting transfers between devices: 3.57 us -> 0 us
    dot_general x32 -> x0, matrix products: 47.9 us -> none  [the longest x16 39.2 us: local_partial(): jnp.einsum('rkgd,lkd->rkgl', head_rows, key_heads, preferred_element_type...]
    all_gather x1 -> x0, blocking collectives: 24.8 us -> none  [shards(): everyone = lax.all_gather(queries, 'slab', axis=0, tiled=True)]
    pallas_call x0 -> x1, Pallas kernels: none -> 23.8 us  [shards(): pl.pallas_call(functools.partial(kernel, n), out_shape=(jax.ShapeDtypeStr...]
    all_to_all x2 -> x0, blocking collectives: 17.9 us -> none  [the longest x1 8.97 us: shards(): lax.all_to_all(part_total, 'slab', split_axis=0, concat_axis=0, tiled=True)]
    all_to_all x1 -> x0, waiting for transfers between devices: 13.8 us -> none  [shards(): lax.all_to_all(part_sum, 'slab', split_axis=0, concat_axis=0, tiled=True)]
    dynamic_update_slice x32 -> x0, local copies, waits for them, and re-layouts: 10 us -> none  [shards(): part_max, part_total, part_sum = lax.map(per_owner, (grouped, owner_bias))]
    unnamed x0 -> x10, local copies, waits for them, and re-layouts: none -> 5.78 us
    reduce_sum x18 -> x0, other arithmetic: 4 us -> none  [the longest x16 3.19 us: local_partial(): row_total = jnp.sum(weights, axis=-1)]
  transfers between devices with their start and end apart: 1 -> 0, of which waited for: 1 -> 0; matrix products, arithmetic and copies ran while one was open for 0% -> 0% of each run, Pallas kernels for 0% -> 0%
where the time goes in v1:
time: 30.6 us; the launch traced here: 30.3 us
  Pallas kernels  23.8 us (78%)
  local copies, waits for them, and re-layouts  5.78 us (19%)
  between operations  0.65 us (2%)
    pallas_call x1, Pallas kernels, shards(): pl.pallas_call(functools.partial(kernel, n), out_shape=(jax.ShapeDtypeStr...  23.8 us
    unnamed x10, local copies, waits for them, and re-layouts  5.78 us

profile of v1, /device:TPU:0, one launch (start us, length us, event | category | flops | bytes accessed | tf_op | source)
XLA Modules:
  0.0 30.3 jit_solution(2533476319103154448)
XLA Ops:
  0.6 0.0 copy-start
  0.6 1.6 %copy-done = bf16[1024,1024]{1,0:T(8,128)(2,1)S(1)} copy-done((bf16[1024,1024]{1,0:T(8,128)(2,1)S(1)}, bf16[1024,1024]{1,0:T(8,128)(2,1)}, u32[]{:S(2)}) %copy-start) | copy-done | bytes 2097176
  2.2 0.0 copy-start.1
  2.2 1.6 %copy-done.1 = bf16[1024,1024]{1,0:T(8,128)(2,1)S(1)} copy-done((bf16[1024,1024]{1,0:T(8,128)(2,1)S(1)}, bf16[1024,1024]{1,0:T(8,128)(2,1)}, u32[]{:S(2)}) %copy-start.1) | copy-done | bytes 2097176
  3.8 0.0 copy-start.2
  3.8 0.8 %copy-done.2 = bf16[1,8192]{1,0:T(2,128)(2,1)S(1)} copy-done((bf16[1,8192]{1,0:T(2,128)(2,1)S(1)}, bf16[1,8192]{1,0:T(2,128)(2,1)}, u32[]{:S(2)}) %copy-start.2) | copy-done | bytes 16408
  4.6 0.0 copy-start.3
  4.6 0.7 %copy-done.3 = s32[16,32]{1,0:T(8,128)S(1)} copy-done((s32[16,32]{1,0:T(8,128)S(1)}, s32[16,32]{1,0:T(8,128)}, u32[]{:S(2)}) %copy-start.3) | copy-done | bytes 2072
  5.3 23.8 %shard_map.59 = (bf16[64,128]{1,0:T(8,128)(2,1)S(1)}, f32[1,64]{1,0:T(1,128)S(1)}) custom-call(bf16[1,8192]{1,0:T(2,128)(2,1)S(1)} %copy-done.2, bf16[1024,1024]{1,0:T(8,128)(2,1)S(1)} %copy-done, bf16[1024,1024]{1,0:T(8,128)(2,1)S(1)} %copy-done.1, s32[16,32]{1,0:T(8,128)S(1)} %copy-done.3), custom_call_target="tpu_custom_call" | custom-call | flops 1073741824 | bytes 4194304 | tf_op jit(solution)/shard_map/pallas_call | solution.py:193
  29.1 0.6 %copy.8 = bf16[1,1,64,128]{3,1,2,0:T(2,128)(2,1)} copy(bf16[1,1,64,128]{3,2,1,0:T(8,128)(2,1)S(1)} %bitcast.5) | data formatting | bytes 32768
  29.8 0.5 %copy.10 = f32[1,64]{1,0:T(1,128)} copy(f32[1,64]{1,0:T(1,128)S(1)} %get-tuple-element.9) | data formatting | bytes 512
Async XLA Ops:
  0.6 1.6 %copy-start = (bf16[1024,1024]{1,0:T(8,128)(2,1)S(1)}, bf16[1024,1024]{1,0:T(8,128)(2,1)}, u32[]{:S(2)}) copy-start(bf16[1024,1024]{1,0:T(8,128)(2,1)} %k_hbm.1) | copy-start | bytes 6291460
  2.2 1.6 %copy-start.1 = (bf16[1024,1024]{1,0:T(8,128)(2,1)S(1)}, bf16[1024,1024]{1,0:T(8,128)(2,1)}, u32[]{:S(2)}) copy-start(bf16[1024,1024]{1,0:T(8,128)(2,1)} %v_hbm.1) | copy-start | bytes 6291460
  3.8 0.8 %copy-start.2 = (bf16[1,8192]{1,0:T(2,128)(2,1)S(1)}, bf16[1,8192]{1,0:T(2,128)(2,1)}, u32[]{:S(2)}) copy-start(bf16[1,8192]{1,0:T(2,128)(2,1)} %q_hbm.1) | copy-start | bytes 49156
  4.6 0.7 %copy-start.3 = (s32[16,32]{1,0:T(8,128)S(1)}, s32[16,32]{1,0:T(8,128)}, u32[]{:S(2)}) copy-start(s32[16,32]{1,0:T(8,128)} %ids_hbm.1) | copy-start | bytes 6148

commit v2 on v1

v2 whole, which is shorter than its diff:
```python
import functools
import math

import jax
import jax.numpy as jnp
from jax import lax
from jax.experimental import pallas as pl
from jax.experimental.pallas import tpu as pltpu
from jax.sharding import PartitionSpec as P

HD = 128
BLOCK = 128
SUB = 8
TILE = 16
CHUNK = 8
MESH = pl.DeviceIdType.MESH

masked_score = -1e30


def kernel(
    n, q_hbm, k_hbm, v_hbm, ids_hbm, att_ref, log_ref,
    q_raw, ids, kbuf, vbuf, held, bias, give, pre, out, got,
    load_sem, q_send, q_recv, f_send, f_recv, p_send, p_recv, o_send, o_recv,
):
    me = lax.axis_index("slab")
    half = n // 2
    core = lax.rem(me, 2)
    other = 1 - core
    spot = me // 2
    sibling = me + 1 - 2 * core
    heads = held.shape[2]
    kv_heads = kbuf.shape[1] // HD
    pairs = heads // TILE
    span = kbuf.shape[0]
    blocks_here = span // BLOCK
    chunk = min(CHUNK, half)
    chunks = half // chunk
    factor = 1.0 / math.sqrt(HD)
    factor2 = factor * math.log2(math.e)

    barrier = pltpu.get_barrier_semaphore()

    @pl.loop(1, n)
    def _(i):
        peer = lax.rem(me + i, n)
        pl.semaphore_signal(barrier, inc=1, device_id={"slab": peer}, device_id_type=MESH)

    loads = [
        pltpu.make_async_copy(src, dst, load_sem.at[at])
        for at, (src, dst) in enumerate(((q_hbm, q_raw), (ids_hbm, ids), (k_hbm, kbuf), (v_hbm, vbuf)))
    ]
    for load in loads:
        load.start()

    loads[0].wait()
    row = q_raw[...].astype(jnp.float32)
    held[core, spot] = jnp.concatenate(
        [row[:, h * HD : (h + 1) * HD] for h in range(heads)], axis=0
    ).astype(jnp.bfloat16)

    def remote(src, dst, send, recv, peer):
        return pltpu.make_async_remote_copy(
            src_ref=src, dst_ref=dst, send_sem=send, recv_sem=recv,
            device_id={"slab": peer}, device_id_type=MESH,
        )

    def spot_at(i):
        return lax.rem(spot + i, half)

    pl.semaphore_wait(barrier, n - 1)

    @pl.loop(1, half)
    def _(i):
        own = held.at[core, spot]
        remote(own, own, q_send, q_recv.at[spot], spot_at(i) * 2 + core).start()

    def forward(at):
        remote(held.at[core, at], held.at[core, at], f_send, f_recv, sibling).start()

    forward(spot)

    loads[1].wait()

    def each_chunk(body):
        if chunks == 1:
            body(0)
        else:
            pl.loop(0, chunks)(body)

    def fill_bias(c):
        rows = pl.ds(c * chunk, chunk)
        both = ids[pl.ds(c * 2 * chunk, 2 * chunk)]
        wide = jnp.broadcast_to(both[:, None, :], (2 * chunk, SUB, ids.shape[1]))
        for j in range(blocks_here):
            hit = jnp.where(wide == me * blocks_here + j, 0.0, masked_score)
            hit = jnp.broadcast_to(jnp.max(hit, axis=-1, keepdims=True), (2 * chunk, SUB, BLOCK))
            hit = hit.reshape(chunk, 2, SUB, BLOCK)
            for side in range(2):
                bias[side, rows, :, j * BLOCK : (j + 1) * BLOCK] = hit[:, side]

    each_chunk(fill_bias)

    @pl.loop(1, half)
    def _(i):
        at = spot_at(half - i)
        remote(held.at[core, at], held.at[core, at], q_send, q_recv.at[at], sibling).wait_recv()
        forward(at)

    loads[2].wait()
    loads[3].wait()

    lane = lax.broadcasted_iota(jnp.int32, (chunk, SUB, HD), 2)
    sub = lax.broadcasted_iota(jnp.int32, (chunk * TILE, HD), 0)
    first = (lax.rem(sub, TILE) < SUB).astype(jnp.float32).astype(jnp.bfloat16)
    second = (lax.rem(sub, TILE) >= SUB).astype(jnp.float32).astype(jnp.bfloat16)

    def partial(side, rows, p):
        rows16 = slice(TILE * p, TILE * (p + 1))
        cols = slice(2 * HD * p, 2 * HD * (p + 1))
        q = held[side, rows, rows16, :].reshape(chunk * TILE, HD)
        q = jnp.concatenate([q * first, q * second], axis=1)
        scores = lax.dot_general(
            q, kbuf[:, cols], (((1,), (1,)), ((), ())), preferred_element_type=jnp.float32
        ).reshape(chunk, 2, SUB, span)
        scores = scores + bias[side, rows][:, None]
        peak = jnp.max(scores, axis=-1, keepdims=True)
        weights = jnp.exp2((scores - peak) * factor2)
        total = jnp.sum(weights, axis=-1, keepdims=True)
        mixed = jnp.dot(
            weights.astype(jnp.bfloat16).reshape(chunk * TILE, span), vbuf[:, cols],
            preferred_element_type=jnp.float32,
        ).reshape(chunk, 2, SUB, 2 * HD)
        mixed = [mixed[:, 0, :, :HD] / total[:, 0], mixed[:, 1, :, HD:] / total[:, 1]]
        logs = peak * factor + jnp.log(total)
        return mixed, [logs[:, 0], logs[:, 1]]

    def put(ref, rows, p, mixed):
        mixed = jnp.concatenate([part[:, None] for part in mixed], axis=1)
        ref[rows, TILE * p : TILE * (p + 1), :] = mixed.reshape(chunk, TILE, HD).astype(jnp.bfloat16)

    def put_logs(ref, rows, columns):
        logs = jnp.zeros((chunk, SUB, HD), jnp.float32)
        for k, column in enumerate(columns):
            logs = jnp.where(lax.rem(lane, kv_heads) == k, column, logs)
        high = logs.astype(jnp.bfloat16).astype(jnp.float32)
        rest = logs - high
        middle = rest.astype(jnp.bfloat16).astype(jnp.float32)
        low = rest - middle
        logs = jnp.where(lane < kv_heads, high, jnp.where(lane < 2 * kv_heads, middle, low))
        logs = jnp.where(lane < 3 * kv_heads, logs, 0.0)
        logs = jnp.concatenate([logs, jnp.zeros_like(logs)], axis=1)
        ref[rows, heads : heads + TILE, :] = logs.astype(jnp.bfloat16)

    def take_logs(ref, rows):
        logs = ref[rows, heads : heads + TILE, :].astype(jnp.float32)[:, :SUB]
        return (
            logs[..., :kv_heads] + logs[..., kv_heads : 2 * kv_heads] + logs[..., 2 * kv_heads : 3 * kv_heads]
        )

    def for_sibling(c):
        rows = pl.ds(c * chunk, chunk)
        columns = []
        for p in range(pairs):
            mixed, logs = partial(core, rows, p)
            put(give, rows, p, mixed)
            columns += logs
        put_logs(give, rows, columns)

    each_chunk(for_sibling)
    to_sibling = remote(give, pre, p_send, p_recv, sibling)
    to_sibling.start()

    whole_side = held.at[other]
    remote(whole_side, whole_side, f_send, f_recv, sibling).wait_recv()
    to_sibling.wait_recv()

    def for_owners(c):
        rows = pl.ds(c * chunk, chunk)
        found = [partial(other, rows, p) for p in range(pairs)]
        theirs = take_logs(pre, rows)
        columns = []
        for p in range(pairs):
            mixed, logs = found[p]
            parts = pre[rows, TILE * p : TILE * (p + 1), :].astype(jnp.float32).reshape(chunk, 2, SUB, HD)
            joined = []
            for at in range(2):
                mine, their = logs[at], theirs[:, :, 2 * p + at : 2 * p + at + 1]
                peak = jnp.maximum(mine, their)
                mine, their = jnp.exp(mine - peak), jnp.exp(their - peak)
                total = mine + their
                joined.append((mixed[at] * mine + parts[:, at] * their) / total)
                columns.append(peak + jnp.log(total))
            put(out, rows, p, joined)
        put_logs(out, rows, columns)

    each_chunk(for_owners)

    @pl.loop(1, half + 1)
    def _(i):
        at = spot_at(i)
        remote(out.at[at], got.at[spot], o_send, o_recv, at * 2 + other).start()

    remote(out, got, o_send, o_recv, sibling).wait_recv()
    logs = take_logs(got, slice(None))
    peak = jnp.max(logs, axis=0)
    shares = jnp.exp(logs - peak[None])
    total = jnp.sum(shares, axis=0)
    shares = shares / total[None]
    joint = peak + jnp.log(total)

    head_lane = lax.broadcasted_iota(jnp.int32, (SUB, heads), 1)
    head_sub = lax.broadcasted_iota(jnp.int32, (SUB, heads), 0)
    spread = jnp.zeros((SUB, heads), jnp.float32)
    for k in range(kv_heads):
        spread = jnp.where(head_lane // SUB == k, joint[:, k : k + 1], spread)
    spread = jnp.where(lax.rem(head_lane, SUB) == head_sub, spread, 0.0)
    log_ref[...] = jnp.sum(spread, axis=0, keepdims=True)

    for p in range(pairs):
        rows16 = slice(TILE * p, TILE * (p + 1))
        parts = got[:, rows16, :].astype(jnp.float32).reshape(half, 2, SUB, HD)
        merged = [
            jnp.sum(parts[:, at] * shares[:, :, 2 * p + at : 2 * p + at + 1], axis=0) for at in range(2)
        ]
        att_ref[rows16, :] = jnp.concatenate(merged, axis=0).astype(jnp.bfloat16)

    sent = held.at[core, pl.ds(0, half - 1)]
    remote(sent, sent, q_send, f_recv, sibling).wait_send()
    remote(whole_side, whole_side, f_send, f_recv, sibling).wait_send()
    to_sibling.wait_send()
    remote(out, got, o_send, o_recv, sibling).wait_send()


def shards(queries, prefix_keys, prefix_values, block_ids):
    n = lax.axis_size("slab")
    rows, width = queries.shape
    span, kv_width = prefix_keys.shape
    heads = width // HD
    half = n // 2
    assert rows == 1 and block_ids.shape[0] == n and heads == SUB * (kv_width // HD) and n % 2 == 0
    anywhere = pl.BlockSpec(memory_space=pltpu.HBM)
    in_vmem = pl.BlockSpec(memory_space=pltpu.VMEM)
    attended, log_totals = pl.pallas_call(
        functools.partial(kernel, n),
        out_shape=(
            pltpu.VMEM((heads, HD), jnp.bfloat16),
            pltpu.VMEM((1, heads), jnp.float32),
        ),
        in_specs=[anywhere] * 4,
        out_specs=(in_vmem, in_vmem),
        scratch_shapes=[
            pltpu.VMEM((1, width), jnp.bfloat16),
            pltpu.VMEM(block_ids.shape, jnp.int32),
            pltpu.VMEM((span, kv_width), jnp.bfloat16),
            pltpu.VMEM((span, kv_width), jnp.bfloat16),
            pltpu.VMEM((2, half, heads, HD), jnp.bfloat16),
            pltpu.VMEM((2, half, SUB, span), jnp.float32),
            pltpu.VMEM((half, heads + TILE, HD), jnp.bfloat16),
            pltpu.VMEM((half, heads + TILE, HD), jnp.bfloat16),
            pltpu.VMEM((half, heads + TILE, HD), jnp.bfloat16),
            pltpu.VMEM((half, heads + TILE, HD), jnp.bfloat16),
            pltpu.SemaphoreType.DMA((4,)),
            pltpu.SemaphoreType.DMA,
            pltpu.SemaphoreType.DMA((half,)),
        ] + [pltpu.SemaphoreType.DMA] * 6,
        compiler_params=pltpu.CompilerParams(
            collective_id=0, has_side_effects=True, vmem_limit_bytes=60 * 1024 * 1024
        ),
        cost_estimate=pl.CostEstimate(
            flops=8 * n * heads * span * HD,
            bytes_accessed=4 * span * kv_width,
            transcendentals=n * heads * span,
        ),
    )(queries, prefix_keys, prefix_values, block_ids)
    return attended.reshape(rows, width), log_totals


def solution(mesh):
    in_specs = (
        P(("groups", "slab"), None),
        P(("groups", "slab"), None),
        P(("groups", "slab"), None),
        P("groups", None),
    )
    out_specs = (P(("groups", "slab"), None), P(("groups", "slab"), None))
    return jax.shard_map(shards, mesh=mesh, in_specs=in_specs, out_specs=out_specs, check_vma=False)
```

time: 30.6 us -> 23 us (0.75)
  local copies, waits for them, and re-layouts: 5.78 us -> 1.15 us
  Pallas kernels: 23.8 us -> 21 us
    unnamed x10 -> x2, local copies, waits for them, and re-layouts: 5.78 us -> 1.15 us
    pallas_call x1, Pallas kernels: 23.8 us -> 21 us  [shards(): pl.pallas_call(functools.partial(kernel, n), out_shape=(pltpu.VMEM((heads...]
where the time goes in v2:
time: 23 us; the launch traced here: 22.8 us
  Pallas kernels  21 us (91%)
  local copies, waits for them, and re-layouts  1.15 us (5%)
  between operations  0.64 us (3%)
    pallas_call x1, Pallas kernels, shards(): pl.pallas_call(functools.partial(kernel, n), out_shape=(pltpu.VMEM((heads...  21 us
    unnamed x2, local copies, waits for them, and re-layouts  1.15 us

profile of v2, /device:TPU:0, one launch (start us, length us, event | category | flops | bytes accessed | tf_op | source)
XLA Modules:
  0.0 22.8 jit_solution(13362854531063693203)
XLA Ops:
  0.6 21.0 %shard_map.59 = (bf16[64,128]{1,0:T(8,128)(2,1)S(1)}, f32[1,64]{1,0:T(1,128)S(1)}) custom-call(bf16[1,8192]{1,0:T(2,128)(2,1)} %q_hbm.1, bf16[1024,1024]{1,0:T(8,128)(2,1)} %k_hbm.1, bf16[1024,1024]{1,0:T(8,128)(2,1)} %v_hbm.1, s32[16,32]{1,0:T(8,128)} %ids_hbm.1), custom_call_target="tpu_custom_call" | custom-call | flops 1073741824 | bytes 4194304 | tf_op jit(solution)/shard_map/pallas_call | solution.py:244
  21.7 0.5 %copy.10 = f32[1,64]{1,0:T(1,128)} copy(f32[1,64]{1,0:T(1,128)S(1)} %get-tuple-element.7) | data formatting | bytes 512
  22.2 0.6 %copy.8 = bf16[1,1,64,128]{3,1,2,0:T(2,128)(2,1)} copy(bf16[1,1,64,128]{3,2,1,0:T(8,128)(2,1)S(1)} %bitcast.5) | data formatting | bytes 32768
